TPU v7x, 256 devices: a whole 4x4x8 slice. The times are simulated.
256 devices in a mesh: region: 32 (over x, z_lo, y), tm: 8 (over z_hi, core).
Axes of the slice: x: 4, y: 4, z: 8 (z_hi: 4, z_lo: 2; z = z_hi * 2 + z_lo), core: 2. Of those that a mesh axis runs over, the one named last changes fastest.
Arguments:
- latents: bfloat16 [32, 1024, 768], P('region', 'tm')
- output_grad: bfloat16 [32, 1024, 768], P('region', 'tm'), may hold values from -6 to 6
- conv_kernel: float32 [4, 768], replicated, may hold values from -1 to 1
- w_query: bfloat16 [768, 768], replicated, may hold values from -0.21875 to 0.21875
- w_key: bfloat16 [768, 768], replicated, may hold values from -0.21875 to 0.21875
- w_value: bfloat16 [768, 768], replicated, may hold values from -0.21875 to 0.21875
- w_out: bfloat16 [768, 768], replicated, may hold values from -0.21875 to 0.21875
- live_counts: int32 [32, 8], P('region', 'tm'), may hold values from 1 to 128, as said below
Outputs:
- input_grad: bfloat16 [32, 1024, 768], P('region', 'tm')
Inputs may be any that keep to these rules, and one draw needn't show every extreme that they name: The first live_counts[r, c] of the 128 tokens of region r in span c are valid.
All inputs are finite; a program needn't handle non-finite values.
Results may differ from a plain program's by a relative error of at most 0.018.
The roundings to bfloat16 on the way count: a program that leaves them out, or rounds other values in their place, can miss the bound.
Values may be sent and summed in bfloat16 or wider, within the bound.
No kernel may reach another device: no remote copies, remote signals or barrier semaphores. Data moves between devices by JAX's collectives and lax.ppermute only.
A program may use at most 128 MiB of HBM per device.

v0:
```python
import math

import jax
import jax.numpy as jnp
from jax import lax
from jax.experimental import pallas as pl
from jax.experimental.pallas import tpu as pltpu
from jax.sharding import PartitionSpec as P

H = 12
HD = 64
KW = 4
WAYS = 2
BLOCK = 16
KEY_STEP = 512
QUERY_STEP = 1024
QUERY_WIDTHS = (512, 768, 1024)
MASKED = -1e30
HEADS_STEP = 4
BF16 = jnp.bfloat16
F32 = jnp.float32


def passed_along(block, axis, distance):
    devices = range(lax.axis_size(axis))
    route = [(i - distance, i) for i in devices if i - distance in devices]
    return lax.ppermute(block, axis, route)


def times(left, right):
    return lax.dot_general(left, right, (((1,), (0,)), ((), ())), preferred_element_type=F32)


def times_back(left, right):
    return lax.dot_general(left, right, (((1,), (1,)), ((), ())), preferred_element_type=F32)


def vmem():
    return pl.BlockSpec(memory_space=pltpu.VMEM)


def smem():
    return pl.BlockSpec(memory_space=pltpu.SMEM)


def fixed(*shape):
    return pl.BlockSpec(shape, lambda i: (0,) * len(shape))


def params(mebibytes):
    return pltpu.CompilerParams(vmem_limit_bytes=mebibytes * 1024 * 1024)


def project_kernel(
    region_ref, live_ref, latents_hbm, edge_hbm, grad_hbm, taps_hbm, wq_hbm, wk_hbm, wv_hbm, wo_hbm, send_hbm,
    latents_ref, edge_ref, grad_ref, taps_ref, wq_ref, wk_ref, wv_ref, wo_ref, send_ref, qg_ref, in_sems, out_sems
):
    span = latents_ref.shape[0]
    columns = HEADS_STEP * HD
    dests = HEADS_STEP * WAYS
    steps = H // HEADS_STEP
    region, live = region_ref[0], live_ref[0, 0]
    small = [
        pltpu.make_async_copy(source, target, in_sems.at[index])
        for index, (source, target) in enumerate(
            ((latents_hbm, latents_ref), (edge_hbm, edge_ref), (taps_hbm, taps_ref), (grad_hbm, grad_ref))
        )
    ]
    weights = []
    for step in range(steps):
        cut = slice(step * columns, (step + 1) * columns)
        parts = [(source.at[:, cut], target.at[step]) for source, target in ((wq_hbm, wq_ref), (wk_hbm, wk_ref), (wv_hbm, wv_ref))]
        parts.append((wo_hbm.at[cut, :], wo_ref.at[step]))
        weights.append(
            [pltpu.make_async_copy(*part, in_sems.at[4 + 4 * step + index]) for index, part in enumerate(parts)]
        )
    for move in small:
        move.start()
    for group in weights:
        for move in group:
            move.start()
    for move in small[:3]:
        move.wait()
    extended = jnp.concatenate([edge_ref[...].astype(F32), latents_ref[...].astype(F32)], axis=0)
    convolved = jnp.zeros(latents_ref.shape, F32)
    for offset in range(KW):
        start = KW - 1 - offset
        convolved = convolved + taps_ref[offset : offset + 1, :] * extended[start : start + span, :]
    hidden = convolved.astype(BF16)
    alive = lax.broadcasted_iota(jnp.int32, (span, 1), 0) < live
    small[3].wait()
    given = grad_ref[...]
    leaving = []
    for step in range(steps):
        for move in weights[step]:
            move.wait()
        queries = (times(hidden, wq_ref[step]).astype(BF16).astype(F32) * (1.0 / math.sqrt(HD))).astype(BF16)
        keys = jnp.where(alive, times(hidden, wk_ref[step]), jnp.nan).astype(BF16)
        values = jnp.where(alive, times(hidden, wv_ref[step]), jnp.nan).astype(BF16)
        grads = (times_back(given, wo_ref[step]) * alive.astype(F32)).astype(BF16)
        for head in range(HEADS_STEP):
            cut = slice(head * HD, (head + 1) * HD)
            pair = jnp.concatenate([keys[:, cut], values[:, cut]], axis=1)
            qg_ref[head] = jnp.concatenate([queries[:, cut], grads[:, cut]], axis=1)
            first = step * dests + head * WAYS
            for half in range(WAYS):
                send_ref[first + half, :span, :] = pair
            for block in range(span // BLOCK):
                half = lax.rem(block + region, WAYS)
                to = span + (block // WAYS) * BLOCK
                send_ref[first + half, to : to + BLOCK, :] = qg_ref[head, block * BLOCK : (block + 1) * BLOCK, :]
        there = slice(step * dests, (step + 1) * dests)
        move = pltpu.make_async_copy(send_ref.at[there], send_hbm.at[there], out_sems.at[step])
        move.start()
        leaving.append(move)
    for move in leaving:
        move.wait()


def attend_kernel(
    region_ref,
    recv_ref,
    send_ref,
    kaug_ref,
    kv_ref,
    kt_ref,
    qg_ref,
    qa_ref,
    gm_ref,
    p_ref,
    wg_ref,
    top_ref,
    dkv_ref,
    dq_ref,
    koff_ref,
    qoff_ref,
):
    regions = recv_ref.shape[0]
    share = recv_ref.shape[1] // (WAYS + 1)
    span = share * WAYS
    me = region_ref[0]
    half = lax.rem(me, WAYS)
    busy = me < H * WAYS
    lane = lax.broadcasted_iota(jnp.int32, (BLOCK, 2 * HD), 1)
    row = lax.broadcasted_iota(jnp.int32, (BLOCK, 2 * HD), 0)
    low = (lax.broadcasted_iota(jnp.int32, (1, 2 * HD), 1) < HD).astype(BF16)
    high = (lax.broadcasted_iota(jnp.int32, (1, 2 * HD), 1) >= HD).astype(BF16)
    mark = (lax.broadcasted_iota(jnp.int32, (1, 2 * HD), 1) == HD).astype(BF16)
    lives = []
    for region in range(regions):
        there = recv_ref[region, :span, :].astype(F32)
        rows_live = jnp.sum((there == there).astype(F32)) * (1.0 / (2 * HD))
        lives.append(jnp.where(busy, jnp.clip(rows_live.astype(jnp.int32), 0, span), 0))
    key_total = query_total = jnp.int32(0)
    for region in range(regions):
        live = lives[region]
        koff_ref[region] = key_total
        qoff_ref[region] = query_total
        pair = recv_ref[region, :span, :]
        here = pl.ds(pl.multiple_of(key_total, BLOCK), span)
        kv_ref[here, :] = pair
        kaug_ref[here, :] = pair * low
        whole = lax.div(live, BLOCK)
        edge = pl.ds(pl.multiple_of(key_total + whole * BLOCK, BLOCK), BLOCK)
        good = row < live - whole * BLOCK
        bias = jnp.where(lane == HD, MASKED, 0.0)
        tail = kv_ref[edge, :].astype(F32)
        kv_ref[edge, :] = jnp.where(good, tail, 0.0).astype(BF16)
        kaug_ref[edge, :] = jnp.where(good, jnp.where(lane < HD, tail, 0.0), bias).astype(BF16)
        both = recv_ref[region, span : span + share, :]
        to = pl.ds(pl.multiple_of(query_total, BLOCK), share)
        qg_ref[to, :] = both
        qa_ref[to, :] = both * low + mark
        gm_ref[to, :] = both * high
        blocks = lax.div(live + BLOCK - 1, BLOCK)
        mine = lax.div(blocks + 1 - lax.rem(half + region, WAYS), WAYS)
        key_total += blocks * BLOCK
        query_total += mine * BLOCK
    rest = pl.ds(pl.multiple_of(key_total, BLOCK), KEY_STEP)
    none = jnp.zeros((KEY_STEP, 2 * HD), BF16)
    kv_ref[rest, :] = none
    kaug_ref[rest, :] = none + mark * MASKED
    rest = pl.ds(pl.multiple_of(query_total, BLOCK), QUERY_STEP)
    none = jnp.zeros((QUERY_STEP, 2 * HD), BF16)
    qg_ref[rest, :] = none
    qa_ref[rest, :] = none
    gm_ref[rest, :] = none
    key_steps = lax.div(key_total + KEY_STEP - 1, KEY_STEP)

    def turn(step, carry):
        keys = kaug_ref[pl.ds(pl.multiple_of(step * KEY_STEP, KEY_STEP), KEY_STEP), :]
        dkv_ref[pl.ds(pl.multiple_of(step * KEY_STEP, KEY_STEP), KEY_STEP), :] = jnp.zeros((KEY_STEP, 2 * HD), F32)
        kt_ref[step] = keys.astype(F32).T[:HD, :].astype(BF16)
        return carry

    lax.fori_loop(0, key_steps, turn, 0)

    def query_block(start, wide):
        at = pl.ds(pl.multiple_of(start, BLOCK), wide)

        def gather(step, state):
            top, total, dot = state
            here = pl.ds(pl.multiple_of(step * KEY_STEP, KEY_STEP), KEY_STEP)
            logits = times_back(kaug_ref[here, :], qa_ref[at, :]).reshape(KEY_STEP // 8, 8, wide)
            weight_grad = times_back(kv_ref[here, :], gm_ref[at, :]).reshape(KEY_STEP // 8, 8, wide)
            new_top = jnp.maximum(top, jnp.max(logits, axis=0))
            shrink = jnp.exp(top - new_top)
            raised = jnp.exp(logits - new_top[None])
            p_ref[step, :, :, :wide] = raised
            wg_ref[step, :, :, :wide] = weight_grad
            top_ref[step, :, :wide] = new_top
            total = total * shrink + jnp.sum(raised, axis=0)
            dot = dot * shrink + jnp.sum(raised * weight_grad, axis=0)
            return (new_top, total, dot)

        none = jnp.zeros((8, wide), F32)
        top, total, dot = lax.fori_loop(0, key_steps, gather, (none + MASKED, none, none))
        best = jnp.max(top, axis=0, keepdims=True)
        shrink = jnp.exp(top - best)
        whole = jnp.sum(total * shrink, axis=0, keepdims=True)
        inverse = 1.0 / whole
        delta = jnp.sum(dot * shrink, axis=0, keepdims=True) * inverse

        def spread(step, query_grad):
            here = pl.ds(pl.multiple_of(step * KEY_STEP, KEY_STEP), KEY_STEP)
            factor = jnp.exp(top_ref[step, :, :wide] - best) * inverse
            attention = p_ref[step, :, :, :wide] * factor[None]
            score_grad = attention * (wg_ref[step, :, :, :wide] - delta[None])
            attention = attention.reshape(KEY_STEP, wide).astype(BF16)
            score_grad = score_grad.reshape(KEY_STEP, wide).astype(BF16)
            both = qg_ref[at, :]
            lane = lax.broadcasted_iota(jnp.int32, (KEY_STEP, 2 * HD), 1)
            dkv_ref[here, :] += jnp.where(lane < HD, times(score_grad, both), times(attention, both))
            return query_grad + times(kt_ref[step], score_grad)

        query_grad = lax.fori_loop(0, key_steps, spread, jnp.zeros((HD, wide), F32))
        query_grad = query_grad * (1.0 / math.sqrt(HD))
        dq_ref[at, :] = jnp.concatenate([query_grad, query_grad], axis=0).T

    full = lax.div(query_total, QUERY_STEP)
    left = query_total - full * QUERY_STEP
    for index, wide in enumerate(QUERY_WIDTHS):
        above = QUERY_WIDTHS[index - 1] if index else 0

        @pl.when((left > above) & (left <= wide))
        def _(wide=wide):
            query_block(full * QUERY_STEP, wide)

    def whole_block(block, carry):
        query_block(block * QUERY_STEP, QUERY_STEP)
        return carry

    lax.fori_loop(0, full, whole_block, 0)

    lane = lax.broadcasted_iota(jnp.int32, (share // 2, 2 * HD), 1)
    for region in range(regions):
        here = pl.ds(pl.multiple_of(koff_ref[region], BLOCK), span)
        send_ref[region, :span, :] = dkv_ref[here, :].astype(BF16)
        first = dq_ref[pl.ds(pl.multiple_of(qoff_ref[region], BLOCK), share // 2), :]
        second = dq_ref[pl.ds(pl.multiple_of(qoff_ref[region] + share // 2, BLOCK), share // 2), :]
        send_ref[region, span:, :] = jnp.where(lane < HD, first, second).astype(BF16)


def return_kernel(
    region_ref, live_ref, recv_ref, taps_ref, wq_ref, wk_ref, wv_ref, out_ref, first_ref, last_ref,
    dk_ref, dv_ref, dq_ref, total_ref
):
    span, width = total_ref.shape[0] - 8, total_ref.shape[1]
    quarter = span // WAYS // 2
    region, live = region_ref[0], live_ref[0, 0]
    alive = lax.broadcasted_iota(jnp.int32, (span, 1), 0) < live
    for duo in range(HEADS_STEP // 2):
        cut = slice(duo * 2 * HD, (duo + 1) * 2 * HD)
        left, right = 2 * duo * WAYS, (2 * duo + 1) * WAYS
        first = recv_ref[left, :span, :].astype(F32) + recv_ref[left + 1, :span, :].astype(F32)
        second = recv_ref[right, :span, :].astype(F32) + recv_ref[right + 1, :span, :].astype(F32)
        key_grad = jnp.concatenate([first[:, :HD], second[:, :HD]], axis=1)
        value_grad = jnp.concatenate([first[:, HD:], second[:, HD:]], axis=1)
        dk_ref[:, cut] = jnp.where(alive, key_grad, 0.0).astype(BF16)
        dv_ref[:, cut] = jnp.where(alive, value_grad, 0.0).astype(BF16)
        for half in range(WAYS):
            shift = lax.rem(half + region, WAYS)
            one = recv_ref[left + half, span:, :].astype(F32)
            two = recv_ref[right + half, span:, :].astype(F32)
            low = jnp.concatenate([one[:, :HD], two[:, :HD]], axis=1)
            high = jnp.concatenate([one[:, HD:], two[:, HD:]], axis=1)
            for number, part in enumerate((low, high)):
                for piece in range(quarter // BLOCK):
                    index = number * (quarter // BLOCK) + piece
                    to = pl.multiple_of((WAYS * index + shift) * BLOCK, BLOCK)
                    dq_ref[pl.ds(to, BLOCK), cut] = part[piece * BLOCK : (piece + 1) * BLOCK, :]
    query_grad = jnp.where(alive, dq_ref[...], 0.0).astype(BF16)
    term = times_back(query_grad, wq_ref[...]) + (
        times_back(dk_ref[...], wk_ref[...]) + times_back(dv_ref[...], wv_ref[...])
    )
    step = pl.program_id(0)

    @pl.when(step == 0)
    def _():
        total_ref[:span, :] = term

    @pl.when(step > 0)
    def _():
        total_ref[:span, :] += term

    @pl.when(step == pl.num_programs(0) - 1)
    def _():
        total_ref[span:, :] = jnp.zeros((8, width), F32)
        input_grad = jnp.zeros((span, width), F32)
        for offset in range(KW):
            input_grad = input_grad + taps_ref[offset : offset + 1, :] * total_ref[offset : offset + span, :]
        out_ref[...] = input_grad.astype(BF16)
        last_ref[...] = input_grad[span - BLOCK :, :]
        first_ref[...] = total_ref[:8, :]


def finish_kernel(last_ref, later_ref, taps_ref, whole_ref, out_ref):
    del whole_ref
    rows, width = last_ref.shape
    total = last_ref[...]
    for offset in range(1, KW):
        reach = jnp.concatenate([jnp.zeros((rows - offset, width), F32), later_ref[:offset, :]], axis=0)
        total = total + taps_ref[offset : offset + 1, :] * reach
    out_ref[...] = total.astype(BF16)


def attend_call(region, gathered):
    regions, rows, _ = gathered.shape
    share = rows // (WAYS + 1)
    span = share * WAYS
    keys, queries = regions * span, regions * share
    key_steps = -(-keys // KEY_STEP)
    return pl.pallas_call(
        attend_kernel,
        name="attend",
        out_shape=jax.ShapeDtypeStruct((regions, span + share // 2, 2 * HD), BF16),
        in_specs=[smem(), vmem()],
        out_specs=vmem(),
        scratch_shapes=[
            pltpu.VMEM((keys + KEY_STEP, 2 * HD), BF16),
            pltpu.VMEM((keys + KEY_STEP, 2 * HD), BF16),
            pltpu.VMEM((key_steps, HD, KEY_STEP), BF16),
            pltpu.VMEM((queries + QUERY_STEP, 2 * HD), BF16),
            pltpu.VMEM((queries + QUERY_STEP, 2 * HD), BF16),
            pltpu.VMEM((queries + QUERY_STEP, 2 * HD), BF16),
            pltpu.VMEM((key_steps, KEY_STEP // 8, 8, QUERY_STEP), F32),
            pltpu.VMEM((key_steps, KEY_STEP // 8, 8, QUERY_STEP), F32),
            pltpu.VMEM((key_steps, 8, QUERY_STEP), F32),
            pltpu.VMEM((keys + KEY_STEP, 2 * HD), F32),
            pltpu.VMEM((queries + QUERY_STEP, 2 * HD), F32),
            pltpu.SMEM((regions,), jnp.int32),
            pltpu.SMEM((regions,), jnp.int32),
        ],
        compiler_params=params(50),
    )(region, gathered)


def shards(latents, output_grad, conv_kernel, w_query, w_key, w_value, w_out, live_counts):
    _, span, width = latents.shape
    regions = lax.axis_size("region")
    share = span // WAYS
    region = lax.axis_index("region").astype(jnp.int32).reshape(1)
    edge = passed_along(latents[:, span - (KW - 1) :, :], "tm", 1)
    steps = H // HEADS_STEP
    columns = HEADS_STEP * HD
    by_columns = pl.BlockSpec((width, columns), lambda i: (0, i))
    anywhere = pl.BlockSpec(memory_space=pl.ANY)
    sent = pl.pallas_call(
        project_kernel,
        name="project",
        out_shape=jax.ShapeDtypeStruct((regions, span + share, 2 * HD), BF16),
        in_specs=[smem(), smem()] + [anywhere] * 8,
        out_specs=anywhere,
        scratch_shapes=[
            pltpu.VMEM((span, width), BF16),
            pltpu.VMEM((KW - 1, width), BF16),
            pltpu.VMEM((span, width), BF16),
            pltpu.VMEM((KW, width), F32),
            pltpu.VMEM((steps, width, columns), BF16),
            pltpu.VMEM((steps, width, columns), BF16),
            pltpu.VMEM((steps, width, columns), BF16),
            pltpu.VMEM((steps, columns, width), BF16),
            pltpu.VMEM((H * WAYS, span + share, 2 * HD), BF16),
            pltpu.VMEM((HEADS_STEP, span, 2 * HD), BF16),
            pltpu.SemaphoreType.DMA((4 + 4 * steps,)),
            pltpu.SemaphoreType.DMA((steps,)),
        ],
        compiler_params=params(60),
    )(region, live_counts, latents[0], edge[0], output_grad[0], conv_kernel, w_query, w_key, w_value, w_out)
    gathered = lax.all_to_all(sent, "region", 0, 0, tiled=True)
    grads = attend_call(region, gathered)
    returned = lax.all_to_all(grads, "region", 0, 0, tiled=True)
    partial, first, last = pl.pallas_call(
        return_kernel,
        name="project_back",
        grid=(steps,),
        out_shape=(
            jax.ShapeDtypeStruct((span, width), BF16),
            jax.ShapeDtypeStruct((8, width), F32),
            jax.ShapeDtypeStruct((BLOCK, width), F32),
        ),
        in_specs=[
            smem(),
            smem(),
            pl.BlockSpec((HEADS_STEP * WAYS, span + share // 2, 2 * HD), lambda i: (i, 0, 0)),
            fixed(KW, width),
            by_columns,
            by_columns,
            by_columns,
        ],
        out_specs=(fixed(span, width), fixed(8, width), fixed(BLOCK, width)),
        scratch_shapes=[
            pltpu.VMEM((span, columns), BF16),
            pltpu.VMEM((span, columns), BF16),
            pltpu.VMEM((span, columns), F32),
            pltpu.VMEM((span + 8, width), F32),
        ],
        compiler_params=params(16),
    )(region, live_counts, returned, conv_kernel, w_query, w_key, w_value)
    later = passed_along(first, "tm", -1)
    input_grad = pl.pallas_call(
        finish_kernel,
        name="finish",
        grid=(1,),
        out_shape=jax.ShapeDtypeStruct((span, width), BF16),
        in_specs=[
            fixed(BLOCK, width),
            fixed(8, width),
            fixed(KW, width),
            pl.BlockSpec(memory_space=pl.ANY),
        ],
        out_specs=pl.BlockSpec((BLOCK, width), lambda i: (span // BLOCK - 1, 0)),
        input_output_aliases={3: 0},
        compiler_params=params(4),
    )(last, later, conv_kernel, partial)
    return input_grad[None]


def solution(mesh):
    in_specs = (
        P("region", "tm", None),
        P("region", "tm", None),
        P(),
        P(),
        P(),
        P(),
        P(),
        P("region", "tm"),
    )
    out_specs = P("region", "tm", None)
    return jax.shard_map(shards, mesh=mesh, in_specs=in_specs, out_specs=out_specs, check_vma=False)
```

profile of v0, /device:TPU:1, one launch (start us, length us, event | category | flops | bytes accessed | tf_op | source)
XLA Modules:
  0.0 87.4 jit_solution(12777820892988962177)
XLA Ops:
  0.0 0.7 slice.3
  0.7 6.3 %collective-permute-start = (bf16[1,3,768]{2,1,0:T(4,128)(2,1)S(1)}, bf16[1,3,768]{2,1,0:T(4,128)(2,1)S(1)}, u32[]{:S(2)}, u32[]{:S(2)}) collective-permute-start(bf16[1,3,768]{2,1,0:T(4,128)(2,1)S(1)} %slice.3), channel_id=1, source_target_pairs={{0,1},{1,2},{2,3},{3,4},{4,5},{5,6},{6,7},{8,9},{9,10},{10,11},{11... | collective-permute-start | bytes 13832 | tf_op jit(solution)/shard_map/ppermute | solution.py:27
  7.7 0.1 collective-permute-done
  7.8 0.0 copy-start.4
  7.8 0.6 copy-done.4
  8.3 4.5 %project.1 = bf16[32,192,128]{2,1,0:T(8,128)(2,1)} custom-call(s32[1]{0:T(128)} %bitcast.region_ref, s32[1,1]{1,0:T(1,128)S(6)} %copy.11.live_ref, bf16[128,768]{1,0:T(8,128)(2,1)} %bitcast.5, bf16[3,768]{1,0:T(4,128)(2,1)} %bitcast.7, bf16[128,768]{1,0:T(8,128)(2,1)} %bitcast.6, f32[4,768]{1,0:T(4,128)} %taps_ref.3, bf16[768,768]{1,0:T(8,128)(2,1)} %wq_ref.1, ...), custom_call_target="tpu_custom_call" | custom-call | tf_op jit(solution)/shard_map/project/pallas_call | solution.py:368
  12.8 29.2 %all_to_all.10.recv_ref = bf16[32,192,128]{2,1,0:T(8,128)(2,1)S(1)} all-to-all(bf16[32,192,128]{2,1,0:T(8,128)(2,1)} %project.1), channel_id=1, replica_groups=mesh['region'=32,'tm'=8] {'region'}, dimensions={0} | all-to-all | bytes 3145728 | tf_op jit(solution)/shard_map/all_to_all | solution.py:390
  42.0 0.0 copy-start.2
  42.0 8.4 %attend.1 = bf16[32,160,128]{2,1,0:T(8,128)(2,1)S(1)} custom-call(s32[1]{0:T(128)} %bitcast.region_ref, bf16[32,192,128]{2,1,0:T(8,128)(2,1)S(1)} %all_to_all.10.recv_ref), custom_call_target="tpu_custom_call" | custom-call | tf_op jit(solution)/shard_map/attend/pallas_call | solution.py:333
  50.5 0.0 copy-start
  50.5 0.0 copy-start.1
  50.5 0.0 copy-start.3
  50.5 23.7 %all_to_all.11.recv_ref = bf16[32,160,128]{2,1,0:T(8,128)(2,1)S(1)} all-to-all(bf16[32,160,128]{2,1,0:T(8,128)(2,1)S(1)} %attend.1), channel_id=1, replica_groups=mesh['region'=32,'tm'=8] {'region'}, dimensions={0} | all-to-all | bytes 2621440 | tf_op jit(solution)/shard_map/all_to_all | solution.py:392
  74.2 0.0 copy-done.2
  74.2 0.0 copy-done
  74.2 0.0 copy-done.1
  74.2 0.0 copy-done.3
  74.2 3.0 %project_back.1 = (bf16[128,768]{1,0:T(8,128)(2,1)}, f32[8,768]{1,0:T(8,128)S(1)}, f32[16,768]{1,0:T(8,128)S(1)}) custom-call(s32[1]{0:T(128)} %bitcast.region_ref, s32[1,1]{1,0:T(1,128)S(6)} %copy.11.live_ref, bf16[32,160,128]{2,1,0:T(8,128)(2,1)S(1)} %all_to_all.11.recv_ref, f32[4,768]{1,0:T(4,128)S(1)} %copy-done.3, bf16[768,768]{1,0:T(8,128)(2,1)S(1)} %copy-done, ...), custom_call_target="tpu_custom_call" | custom-call | tf_op jit(solution)/shard_map/project_back/pallas_call | solution.py:393
  77.2 2.2 %collective-permute-start.1 = (f32[8,768]{1,0:T(8,128)S(1)}, f32[8,768]{1,0:T(8,128)S(1)}, u32[]{:S(2)}, u32[]{:S(2)}) collective-permute-start(f32[8,768]{1,0:T(8,128)S(1)} %get-tuple-element.9), channel_id=1, source_target_pairs={{1,0},{2,1},{3,2},{4,3},{5,4},{6,5},{7,6},{9,8},{10,9},{11,10},{12... | collective-permute-start | bytes 73736 | tf_op jit(solution)/shard_map/ppermute | solution.py:27
  79.4 7.3 %collective-permute-done.1.later_ref = f32[8,768]{1,0:T(8,128)S(1)} collective-permute-done((f32[8,768]{1,0:T(8,128)S(1)}, f32[8,768]{1,0:T(8,128)S(1)}, u32[]{:S(2)}, u32[]{:S(2)}) %collective-permute-start.1) | collective-permute-done | bytes 24608 | tf_op jit(solution)/shard_map/ppermute | solution.py:27
  86.8 0.6 finish.1
Async XLA Ops:
  0.7 7.0 %collective-permute-start = (bf16[1,3,768]{2,1,0:T(4,128)(2,1)S(1)}, bf16[1,3,768]{2,1,0:T(4,128)(2,1)S(1)}, u32[]{:S(2)}, u32[]{:S(2)}) collective-permute-start(bf16[1,3,768]{2,1,0:T(4,128)(2,1)S(1)} %slice.3), channel_id=1, source_target_pairs={{0,1},{1,2},{2,3},{3,4},{4,5},{5,6},{6,7},{8,9},{9,10},{10,11},{11... | collective-permute-start | bytes 13832 | tf_op jit(solution)/shard_map/ppermute | solution.py:27
  7.8 0.6 copy-start.4
  42.0 32.2 %copy-start.2 = (bf16[768,768]{1,0:T(8,128)(2,1)S(1)}, bf16[768,768]{1,0:T(8,128)(2,1)}, u32[]{:S(2)}) copy-start(bf16[768,768]{1,0:T(8,128)(2,1)} %wv_ref.1) | copy-start | bytes 3538948
  50.5 23.7 %copy-start = (bf16[768,768]{1,0:T(8,128)(2,1)S(1)}, bf16[768,768]{1,0:T(8,128)(2,1)}, u32[]{:S(2)}) copy-start(bf16[768,768]{1,0:T(8,128)(2,1)} %wq_ref.1) | copy-start | bytes 3538948
  50.5 23.7 %copy-start.1 = (bf16[768,768]{1,0:T(8,128)(2,1)S(1)}, bf16[768,768]{1,0:T(8,128)(2,1)}, u32[]{:S(2)}) copy-start(bf16[768,768]{1,0:T(8,128)(2,1)} %wk_ref.1) | copy-start | bytes 3538948
  50.5 23.7 %copy-start.3 = (f32[4,768]{1,0:T(4,128)S(1)}, f32[4,768]{1,0:T(4,128)}, u32[]{:S(2)}) copy-start(f32[4,768]{1,0:T(4,128)} %taps_ref.3) | copy-start | bytes 36868
  77.2 9.5 %collective-permute-start.1 = (f32[8,768]{1,0:T(8,128)S(1)}, f32[8,768]{1,0:T(8,128)S(1)}, u32[]{:S(2)}, u32[]{:S(2)}) collective-permute-start(f32[8,768]{1,0:T(8,128)S(1)} %get-tuple-element.9), channel_id=1, source_target_pairs={{1,0},{2,1},{3,2},{4,3},{5,4},{6,5},{7,6},{9,8},{10,9},{11,10},{12... | collective-permute-start | bytes 73736 | tf_op jit(solution)/shard_map/ppermute | solution.py:27
where the time goes:
time: 86.4 us; the launch traced here: 87.4 us
  blocking collectives  52.9 us (61%)
  Pallas kernels  16.5 us (19%)
  starting transfers between devices  8.44 us (10%)
  waiting for transfers between devices  7.44 us (9%)
  local copies, waits for them, and re-layouts  1.33 us (2%)
    all_to_all x1, blocking collectives, shards(): gathered = lax.all_to_all(sent, 'region', 0, 0, tiled=True)  29.2 us
    all_to_all x1, blocking collectives, shards(): returned = lax.all_to_all(grads, 'region', 0, 0, tiled=True)  23.7 us
    ppermute x2, starting transfers between devices, passed_along(): return lax.ppermute(block, axis, route)  8.44 us
    pallas_call x1, Pallas kernels, attend_call(): pl.pallas_call(attend_kernel, name='attend', out_shape=jax.ShapeDtypeStru...  8.44 us
    ppermute x2, waiting for transfers between devices, passed_along(): return lax.ppermute(block, axis, route)  7.44 us
    pallas_call x1, Pallas kernels, shards(): pl.pallas_call(project_kernel, name='project', out_shape=jax.ShapeDtypeSt...  4.46 us
    pallas_call x1, Pallas kernels, shards(): pl.pallas_call(return_kernel, name='project_back', grid=(steps,), out_sha...  3.01 us
  transfers between devices with their start and end apart: 2, of which 2 were waited for; matrix products, arithmetic and copies ran while one was open for 0% of the time, Pallas kernels for 0%

commit v1 on v0

--- a/solution.py
+++ b/solution.py
@@ -14,7 +14,7 @@
 BLOCK = 16
 KEY_STEP = 512
 QUERY_STEP = 1024
-QUERY_WIDTHS = (512, 768, 1024)
+QUERY_WIDTHS = (512, 640, 768, 896, 1024)
 MASKED = -1e30
 HEADS_STEP = 4
 BF16 = jnp.bfloat16
@@ -51,9 +51,22 @@
     return pltpu.CompilerParams(vmem_limit_bytes=mebibytes * 1024 * 1024)
 
 
+def grad_kernel(live_ref, grad_hbm, wo_hbm, out_ref, grad_ref, wo_ref, sems):
+    moves = [
+        pltpu.make_async_copy(grad_hbm, grad_ref, sems.at[0]),
+        pltpu.make_async_copy(wo_hbm, wo_ref, sems.at[1]),
+    ]
+    for move in moves:
+        move.start()
+    for move in moves:
+        move.wait()
+    alive = lax.broadcasted_iota(jnp.int32, (out_ref.shape[0], 1), 0) < live_ref[0, 0]
+    out_ref[...] = (times_back(grad_ref[...], wo_ref[...]) * alive.astype(F32)).astype(BF16)
+
+
 def project_kernel(
-    region_ref, live_ref, latents_hbm, edge_hbm, grad_hbm, taps_hbm, wq_hbm, wk_hbm, wv_hbm, wo_hbm, send_hbm,
-    latents_ref, edge_ref, grad_ref, taps_ref, wq_ref, wk_ref, wv_ref, wo_ref, send_ref, qg_ref, in_sems, out_sems
+    region_ref, live_ref, latents_hbm, edge_hbm, grads_hbm, taps_hbm, wq_hbm, wk_hbm, wv_hbm, send_hbm,
+    latents_ref, edge_ref, grads_ref, taps_ref, wq_ref, wk_ref, wv_ref, send_ref, qg_ref, in_sems, out_sems
 ):
     span = latents_ref.shape[0]
     columns = HEADS_STEP * HD
@@ -63,16 +76,15 @@
     small = [
         pltpu.make_async_copy(source, target, in_sems.at[index])
         for index, (source, target) in enumerate(
-            ((latents_hbm, latents_ref), (edge_hbm, edge_ref), (taps_hbm, taps_ref), (grad_hbm, grad_ref))
+            ((latents_hbm, latents_ref), (edge_hbm, edge_ref), (taps_hbm, taps_ref), (grads_hbm, grads_ref))
         )
     ]
     weights = []
     for step in range(steps):
         cut = slice(step * columns, (step + 1) * columns)
         parts = [(source.at[:, cut], target.at[step]) for source, target in ((wq_hbm, wq_ref), (wk_hbm, wk_ref), (wv_hbm, wv_ref))]
-        parts.append((wo_hbm.at[cut, :], wo_ref.at[step]))
         weights.append(
-            [pltpu.make_async_copy(*part, in_sems.at[4 + 4 * step + index]) for index, part in enumerate(parts)]
+            [pltpu.make_async_copy(*part, in_sems.at[4 + 3 * step + index]) for index, part in enumerate(parts)]
         )
     for move in small:
         move.start()
@@ -89,7 +101,7 @@
     hidden = convolved.astype(BF16)
     alive = lax.broadcasted_iota(jnp.int32, (span, 1), 0) < live
     small[3].wait()
-    given = grad_ref[...]
+    given = grads_ref[...]
     leaving = []
     for step in range(steps):
         for move in weights[step]:
@@ -97,7 +109,7 @@
         queries = (times(hidden, wq_ref[step]).astype(BF16).astype(F32) * (1.0 / math.sqrt(HD))).astype(BF16)
         keys = jnp.where(alive, times(hidden, wk_ref[step]), jnp.nan).astype(BF16)
         values = jnp.where(alive, times(hidden, wv_ref[step]), jnp.nan).astype(BF16)
-        grads = (times_back(given, wo_ref[step]) * alive.astype(F32)).astype(BF16)
+        grads = given[:, step * columns : (step + 1) * columns]
         for head in range(HEADS_STEP):
             cut = slice(head * HD, (head + 1) * HD)
             pair = jnp.concatenate([keys[:, cut], values[:, cut]], axis=1)
@@ -269,7 +281,7 @@
     quarter = span // WAYS // 2
     region, live = region_ref[0], live_ref[0, 0]
     alive = lax.broadcasted_iota(jnp.int32, (span, 1), 0) < live
-    for duo in range(HEADS_STEP // 2):
+    for duo in range(H // 2):
         cut = slice(duo * 2 * HD, (duo + 1) * 2 * HD)
         left, right = 2 * duo * WAYS, (2 * duo + 1) * WAYS
         first = recv_ref[left, :span, :].astype(F32) + recv_ref[left + 1, :span, :].astype(F32)
@@ -290,28 +302,16 @@
                     to = pl.multiple_of((WAYS * index + shift) * BLOCK, BLOCK)
                     dq_ref[pl.ds(to, BLOCK), cut] = part[piece * BLOCK : (piece + 1) * BLOCK, :]
     query_grad = jnp.where(alive, dq_ref[...], 0.0).astype(BF16)
-    term = times_back(query_grad, wq_ref[...]) + (
+    total_ref[:span, :] = times_back(query_grad, wq_ref[...]) + (
         times_back(dk_ref[...], wk_ref[...]) + times_back(dv_ref[...], wv_ref[...])
     )
-    step = pl.program_id(0)
-
-    @pl.when(step == 0)
-    def _():
-        total_ref[:span, :] = term
-
-    @pl.when(step > 0)
-    def _():
-        total_ref[:span, :] += term
-
-    @pl.when(step == pl.num_programs(0) - 1)
-    def _():
-        total_ref[span:, :] = jnp.zeros((8, width), F32)
-        input_grad = jnp.zeros((span, width), F32)
-        for offset in range(KW):
-            input_grad = input_grad + taps_ref[offset : offset + 1, :] * total_ref[offset : offset + span, :]
-        out_ref[...] = input_grad.astype(BF16)
-        last_ref[...] = input_grad[span - BLOCK :, :]
-        first_ref[...] = total_ref[:8, :]
+    total_ref[span:, :] = jnp.zeros((8, width), F32)
+    first_ref[...] = total_ref[:8, :]
+    input_grad = jnp.zeros((span, width), F32)
+    for offset in range(KW):
+        input_grad = input_grad + taps_ref[offset : offset + 1, :] * total_ref[offset : offset + span, :]
+    out_ref[...] = input_grad.astype(BF16)
+    last_ref[...] = input_grad[span - BLOCK :, :]
 
 
 def finish_kernel(last_ref, later_ref, taps_ref, whole_ref, out_ref):
@@ -363,13 +363,28 @@
     edge = passed_along(latents[:, span - (KW - 1) :, :], "tm", 1)
     steps = H // HEADS_STEP
     columns = HEADS_STEP * HD
-    by_columns = pl.BlockSpec((width, columns), lambda i: (0, i))
     anywhere = pl.BlockSpec(memory_space=pl.ANY)
+    grad_proj = pl.pallas_call(
+        grad_kernel,
+        name="project_grad",
+        out_shape=jax.ShapeDtypeStruct((span, width), BF16),
+        in_specs=[smem(), anywhere, anywhere],
+        out_specs=vmem(),
+        scratch_shapes=[
+            pltpu.VMEM((span, width), BF16),
+            pltpu.VMEM((width, width), BF16),
+            pltpu.SemaphoreType.DMA((2,)),
+        ],
+        compiler_params=params(60),
+        cost_estimate=pl.CostEstimate(
+            flops=2 * span * width * width, bytes_accessed=2 * width * (width + 2 * span), transcendentals=0
+        ),
+    )(live_counts, output_grad[0], w_out)
     sent = pl.pallas_call(
         project_kernel,
         name="project",
         out_shape=jax.ShapeDtypeStruct((regions, span + share, 2 * HD), BF16),
-        in_specs=[smem(), smem()] + [anywhere] * 8,
+        in_specs=[smem(), smem()] + [anywhere] * 7,
         out_specs=anywhere,
         scratch_shapes=[
             pltpu.VMEM((span, width), BF16),
@@ -379,40 +394,30 @@
             pltpu.VMEM((steps, width, columns), BF16),
             pltpu.VMEM((steps, width, columns), BF16),
             pltpu.VMEM((steps, width, columns), BF16),
-            pltpu.VMEM((steps, columns, width), BF16),
             pltpu.VMEM((H * WAYS, span + share, 2 * HD), BF16),
             pltpu.VMEM((HEADS_STEP, span, 2 * HD), BF16),
-            pltpu.SemaphoreType.DMA((4 + 4 * steps,)),
+            pltpu.SemaphoreType.DMA((4 + 3 * steps,)),
             pltpu.SemaphoreType.DMA((steps,)),
         ],
-        compiler_params=params(60),
-    )(region, live_counts, latents[0], edge[0], output_grad[0], conv_kernel, w_query, w_key, w_value, w_out)
+        compiler_params=params(54),
+    )(region, live_counts, latents[0], edge[0], grad_proj, conv_kernel, w_query, w_key, w_value)
     gathered = lax.all_to_all(sent, "region", 0, 0, tiled=True)
     grads = attend_call(region, gathered)
     returned = lax.all_to_all(grads, "region", 0, 0, tiled=True)
     partial, first, last = pl.pallas_call(
         return_kernel,
         name="project_back",
-        grid=(steps,),
         out_shape=(
             jax.ShapeDtypeStruct((span, width), BF16),
             jax.ShapeDtypeStruct((8, width), F32),
             jax.ShapeDtypeStruct((BLOCK, width), F32),
         ),
-        in_specs=[
-            smem(),
-            smem(),
-            pl.BlockSpec((HEADS_STEP * WAYS, span + share // 2, 2 * HD), lambda i: (i, 0, 0)),
-            fixed(KW, width),
-            by_columns,
-            by_columns,
-            by_columns,
-        ],
-        out_specs=(fixed(span, width), fixed(8, width), fixed(BLOCK, width)),
+        in_specs=[smem(), smem()] + [vmem()] * 5,
+        out_specs=[vmem()] * 3,
         scratch_shapes=[
-            pltpu.VMEM((span, columns), BF16),
-            pltpu.VMEM((span, columns), BF16),
-            pltpu.VMEM((span, columns), F32),
+            pltpu.VMEM((span, width), BF16),
+            pltpu.VMEM((span, width), BF16),
+            pltpu.VMEM((span, width), F32),
             pltpu.VMEM((span + 8, width), F32),
         ],
         compiler_params=params(16),

time: 86.4 us -> 85.6 us (level)
  the two profiles are of different devices: /device:TPU:1 before, /device:TPU:65 now
where the time goes in v1:
time: 85.6 us; the launch traced here: 85.2 us
  blocking collectives  51.4 us (60%)
  Pallas kernels  14.7 us (17%)
  starting transfers between devices  10.9 us (13%)
  waiting for transfers between devices  6.04 us (7%)
  local copies, waits for them, and re-layouts  1.32 us (2%)
    all_to_all x1, blocking collectives, shards(): gathered = lax.all_to_all(sent, 'region', 0, 0, tiled=True)  28.7 us
    all_to_all x1, blocking collectives, shards(): returned = lax.all_to_all(grads, 'region', 0, 0, tiled=True)  22.7 us
    ppermute x2, starting transfers between devices, passed_along(): return lax.ppermute(block, axis, route)  10.9 us
    ppermute x2, waiting for transfers between devices, passed_along(): return lax.ppermute(block, axis, route)  6.04 us
    pallas_call x1, Pallas kernels, attend_call(): pl.pallas_call(attend_kernel, name='attend', out_shape=jax.ShapeDtypeStru...  5.67 us
    pallas_call x1, Pallas kernels, shards(): pl.pallas_call(project_kernel, name='project', out_shape=jax.ShapeDtypeSt...  3.73 us
    pallas_call x1, Pallas kernels, shards(): pl.pallas_call(grad_kernel, name='project_grad', out_shape=jax.ShapeDtype...  2.62 us
    pallas_call x1, Pallas kernels, shards(): pl.pallas_call(return_kernel, name='project_back', out_shape=(jax.ShapeDt...  2.1 us
  transfers between devices with their start and end apart: 2, of which 1 were waited for; matrix products, arithmetic and copies ran while one was open for 0% of the time, Pallas kernels for 3%

profile of v1, /device:TPU:65, one launch (start us, length us, event | category | flops | bytes accessed | tf_op | source)
XLA Modules:
  0.0 85.2 jit_solution(9441489576995440750)
XLA Ops:
  0.0 0.7 slice.3
  0.7 6.7 %collective-permute-start = (bf16[1,3,768]{2,1,0:T(4,128)(2,1)S(1)}, bf16[1,3,768]{2,1,0:T(4,128)(2,1)S(1)}, u32[]{:S(2)}, u32[]{:S(2)}) collective-permute-start(bf16[1,3,768]{2,1,0:T(4,128)(2,1)S(1)} %slice.3), channel_id=1, source_target_pairs={{0,1},{1,2},{2,3},{3,4},{4,5},{5,6},{6,7},{8,9},{9,10},{10,11},{11... | collective-permute-start | bytes 13832 | tf_op jit(solution)/shard_map/ppermute | solution.py:27
  8.0 2.6 %project_grad.1.grads_hbm = bf16[128,768]{1,0:T(8,128)(2,1)} custom-call(s32[1,1]{1,0:T(1,128)S(6)} %copy.11.live_ref, bf16[128,768]{1,0:T(8,128)(2,1)} %bitcast.6, bf16[768,768]{1,0:T(8,128)(2,1)} %wo_hbm.1), custom_call_target="tpu_custom_call" | custom-call | flops 150994944 | bytes 1572864 | tf_op jit(solution)/shard_map/project_grad/pallas_call | solution.py:367
  10.7 0.0 collective-permute-done
  10.7 0.0 copy-start.4
  10.7 0.6 copy-done.4
  11.3 3.7 %project.1 = bf16[32,192,128]{2,1,0:T(8,128)(2,1)} custom-call(s32[1]{0:T(128)} %bitcast.region_ref, s32[1,1]{1,0:T(1,128)S(6)} %copy.11.live_ref, bf16[128,768]{1,0:T(8,128)(2,1)} %bitcast.5, bf16[3,768]{1,0:T(4,128)(2,1)} %bitcast.7, bf16[128,768]{1,0:T(8,128)(2,1)} %project_grad.1.grads_hbm, f32[4,768]{1,0:T(4,128)} %taps_ref.3, bf16[768,768]{1,0:T(8,128)(2,1)} %wq_ref.1, ...), custom_call_target="tpu_custom_call" | custom-call | tf_op jit(solution)/shard_map/project/pallas_call | solution.py:383
  15.0 28.7 %all_to_all.10.recv_ref = bf16[32,192,128]{2,1,0:T(8,128)(2,1)S(1)} all-to-all(bf16[32,192,128]{2,1,0:T(8,128)(2,1)} %project.1), channel_id=1, replica_groups=mesh['region'=32,'tm'=8] {'region'}, dimensions={0} | all-to-all | bytes 3145728 | tf_op jit(solution)/shard_map/all_to_all | solution.py:404
  43.7 0.0 copy-start.2
  43.7 5.7 %attend.1 = bf16[32,160,128]{2,1,0:T(8,128)(2,1)S(1)} custom-call(s32[1]{0:T(128)} %bitcast.region_ref, bf16[32,192,128]{2,1,0:T(8,128)(2,1)S(1)} %all_to_all.10.recv_ref), custom_call_target="tpu_custom_call" | custom-call | tf_op jit(solution)/shard_map/attend/pallas_call | solution.py:333
  49.4 0.0 copy-start
  49.4 0.0 copy-start.1
  49.4 0.0 copy-start.3
  49.4 22.7 %all_to_all.11.recv_ref = bf16[32,160,128]{2,1,0:T(8,128)(2,1)S(1)} all-to-all(bf16[32,160,128]{2,1,0:T(8,128)(2,1)S(1)} %attend.1), channel_id=1, replica_groups=mesh['region'=32,'tm'=8] {'region'}, dimensions={0} | all-to-all | bytes 2621440 | tf_op jit(solution)/shard_map/all_to_all | solution.py:406
  72.1 0.0 copy-done.2
  72.1 0.0 copy-done
  72.1 0.0 copy-done.1
  72.1 0.0 copy-done.3
  72.1 2.1 %project_back.1 = (bf16[128,768]{1,0:T(8,128)(2,1)}, f32[8,768]{1,0:T(8,128)S(1)}, f32[16,768]{1,0:T(8,128)S(1)}) custom-call(s32[1]{0:T(128)} %bitcast.region_ref, s32[1,1]{1,0:T(1,128)S(6)} %copy.11.live_ref, bf16[32,160,128]{2,1,0:T(8,128)(2,1)S(1)} %all_to_all.11.recv_ref, f32[4,768]{1,0:T(4,128)S(1)} %copy-done.3, bf16[768,768]{1,0:T(8,128)(2,1)S(1)} %copy-done, ...), custom_call_target="tpu_custom_call" | custom-call | tf_op jit(solution)/shard_map/project_back/pallas_call | solution.py:407
  74.2 4.2 %collective-permute-start.1 = (f32[8,768]{1,0:T(8,128)S(1)}, f32[8,768]{1,0:T(8,128)S(1)}, u32[]{:S(2)}, u32[]{:S(2)}) collective-permute-start(f32[8,768]{1,0:T(8,128)S(1)} %get-tuple-element.9), channel_id=1, source_target_pairs={{1,0},{2,1},{3,2},{4,3},{5,4},{6,5},{7,6},{9,8},{10,9},{11,10},{12... | collective-permute-start | bytes 73736 | tf_op jit(solution)/shard_map/ppermute | solution.py:27
  78.5 6.0 %collective-permute-done.1.later_ref = f32[8,768]{1,0:T(8,128)S(1)} collective-permute-done((f32[8,768]{1,0:T(8,128)S(1)}, f32[8,768]{1,0:T(8,128)S(1)}, u32[]{:S(2)}, u32[]{:S(2)}) %collective-permute-start.1) | collective-permute-done | bytes 24608 | tf_op jit(solution)/shard_map/ppermute | solution.py:27
  84.5 0.6 finish.1
Async XLA Ops:
  0.7 9.9 %collective-permute-start = (bf16[1,3,768]{2,1,0:T(4,128)(2,1)S(1)}, bf16[1,3,768]{2,1,0:T(4,128)(2,1)S(1)}, u32[]{:S(2)}, u32[]{:S(2)}) collective-permute-start(bf16[1,3,768]{2,1,0:T(4,128)(2,1)S(1)} %slice.3), channel_id=1, source_target_pairs={{0,1},{1,2},{2,3},{3,4},{4,5},{5,6},{6,7},{8,9},{9,10},{10,11},{11... | collective-permute-start | bytes 13832 | tf_op jit(solution)/shard_map/ppermute | solution.py:27
  10.7 0.6 copy-start.4
  43.7 28.4 %copy-start.2 = (bf16[768,768]{1,0:T(8,128)(2,1)S(1)}, bf16[768,768]{1,0:T(8,128)(2,1)}, u32[]{:S(2)}) copy-start(bf16[768,768]{1,0:T(8,128)(2,1)} %wv_ref.1) | copy-start | bytes 3538948
  49.4 22.7 %copy-start = (bf16[768,768]{1,0:T(8,128)(2,1)S(1)}, bf16[768,768]{1,0:T(8,128)(2,1)}, u32[]{:S(2)}) copy-start(bf16[768,768]{1,0:T(8,128)(2,1)} %wq_ref.1) | copy-start | bytes 3538948
  49.4 22.7 %copy-start.1 = (bf16[768,768]{1,0:T(8,128)(2,1)S(1)}, bf16[768,768]{1,0:T(8,128)(2,1)}, u32[]{:S(2)}) copy-start(bf16[768,768]{1,0:T(8,128)(2,1)} %wk_ref.1) | copy-start | bytes 3538948
  49.4 22.7 %copy-start.3 = (f32[4,768]{1,0:T(4,128)S(1)}, f32[4,768]{1,0:T(4,128)}, u32[]{:S(2)}) copy-start(f32[4,768]{1,0:T(4,128)} %taps_ref.3) | copy-start | bytes 36868
  74.2 10.3 %collective-permute-start.1 = (f32[8,768]{1,0:T(8,128)S(1)}, f32[8,768]{1,0:T(8,128)S(1)}, u32[]{:S(2)}, u32[]{:S(2)}) collective-permute-start(f32[8,768]{1,0:T(8,128)S(1)} %get-tuple-element.9), channel_id=1, source_target_pairs={{1,0},{2,1},{3,2},{4,3},{5,4},{6,5},{7,6},{9,8},{10,9},{11,10},{12... | collective-permute-start | bytes 73736 | tf_op jit(solution)/shard_map/ppermute | solution.py:27

commit v2 on v1

--- a/solution.py
+++ b/solution.py
@@ -65,8 +65,8 @@
 
 
 def project_kernel(
-    region_ref, live_ref, latents_hbm, edge_hbm, grads_hbm, taps_hbm, wq_hbm, wk_hbm, wv_hbm, send_hbm,
-    latents_ref, edge_ref, grads_ref, taps_ref, wq_ref, wk_ref, wv_ref, send_ref, qg_ref, in_sems, out_sems
+    region_ref, live_ref, latents_hbm, edge_ref, grads_hbm, taps_hbm, wq_hbm, wk_hbm, wv_hbm, send_hbm,
+    latents_ref, grads_ref, taps_ref, wq_ref, wk_ref, wv_ref, send_ref, qg_ref, in_sems, out_sems
 ):
     span = latents_ref.shape[0]
     columns = HEADS_STEP * HD
@@ -76,7 +76,7 @@
     small = [
         pltpu.make_async_copy(source, target, in_sems.at[index])
         for index, (source, target) in enumerate(
-            ((latents_hbm, latents_ref), (edge_hbm, edge_ref), (taps_hbm, taps_ref), (grads_hbm, grads_ref))
+            ((latents_hbm, latents_ref), (taps_hbm, taps_ref), (grads_hbm, grads_ref))
         )
     ]
     weights = []
@@ -84,14 +84,14 @@
         cut = slice(step * columns, (step + 1) * columns)
         parts = [(source.at[:, cut], target.at[step]) for source, target in ((wq_hbm, wq_ref), (wk_hbm, wk_ref), (wv_hbm, wv_ref))]
         weights.append(
-            [pltpu.make_async_copy(*part, in_sems.at[4 + 3 * step + index]) for index, part in enumerate(parts)]
+            [pltpu.make_async_copy(*part, in_sems.at[3 + 3 * step + index]) for index, part in enumerate(parts)]
         )
     for move in small:
         move.start()
     for group in weights:
         for move in group:
             move.start()
-    for move in small[:3]:
+    for move in small[:2]:
         move.wait()
     extended = jnp.concatenate([edge_ref[...].astype(F32), latents_ref[...].astype(F32)], axis=0)
     convolved = jnp.zeros(latents_ref.shape, F32)
@@ -100,7 +100,7 @@
         convolved = convolved + taps_ref[offset : offset + 1, :] * extended[start : start + span, :]
     hidden = convolved.astype(BF16)
     alive = lax.broadcasted_iota(jnp.int32, (span, 1), 0) < live
-    small[3].wait()
+    small[2].wait()
     given = grads_ref[...]
     leaving = []
     for step in range(steps):
@@ -375,7 +375,7 @@
             pltpu.VMEM((width, width), BF16),
             pltpu.SemaphoreType.DMA((2,)),
         ],
-        compiler_params=params(60),
+        compiler_params=params(53),
         cost_estimate=pl.CostEstimate(
             flops=2 * span * width * width, bytes_accessed=2 * width * (width + 2 * span), transcendentals=0
         ),
@@ -384,11 +384,10 @@
         project_kernel,
         name="project",
         out_shape=jax.ShapeDtypeStruct((regions, span + share, 2 * HD), BF16),
-        in_specs=[smem(), smem()] + [anywhere] * 7,
+        in_specs=[smem(), smem(), anywhere, vmem()] + [anywhere] * 5,
         out_specs=anywhere,
         scratch_shapes=[
             pltpu.VMEM((span, width), BF16),
-            pltpu.VMEM((KW - 1, width), BF16),
             pltpu.VMEM((span, width), BF16),
             pltpu.VMEM((KW, width), F32),
             pltpu.VMEM((steps, width, columns), BF16),
@@ -396,10 +395,10 @@
             pltpu.VMEM((steps, width, columns), BF16),
             pltpu.VMEM((H * WAYS, span + share, 2 * HD), BF16),
             pltpu.VMEM((HEADS_STEP, span, 2 * HD), BF16),
-            pltpu.SemaphoreType.DMA((4 + 3 * steps,)),
+            pltpu.SemaphoreType.DMA((3 + 3 * steps,)),
             pltpu.SemaphoreType.DMA((steps,)),
         ],
-        compiler_params=params(54),
+        compiler_params=params(53),
     )(region, live_counts, latents[0], edge[0], grad_proj, conv_kernel, w_query, w_key, w_value)
     gathered = lax.all_to_all(sent, "region", 0, 0, tiled=True)
     grads = attend_call(region, gathered)

time: 85.6 us -> 85.4 us (level)
  starting transfers between devices: 10.9 us -> 8.82 us
  Pallas kernels: 14.7 us -> 16.7 us
    pallas_call x1, Pallas kernels: 5.67 us -> 7.86 us  [attend_call(): pl.pallas_call(attend_kernel, name='attend', out_shape=jax.ShapeDtypeStru...]
    ppermute x2, starting transfers between devices: 10.9 us -> 8.82 us  [passed_along(): return lax.ppermute(block, axis, route)]
  transfers between devices with their start and end apart: 2 -> 2, of which waited for: 1 -> 1; matrix products, arithmetic and copies ran while one was open for 0% -> 0% of each run, Pallas kernels for 3% -> 2%
where the time goes in v2:
time: 85.4 us; the launch traced here: 85.2 us
  blocking collectives  51.8 us (61%)
  Pallas kernels  16.7 us (20%)
  starting transfers between devices  8.82 us (10%)
  waiting for transfers between devices  5.39 us (6%)
  local copies, waits for them, and re-layouts  1.73 us (2%)
    all_to_all x1, blocking collectives, shards(): gathered = lax.all_to_all(sent, 'region', 0, 0, tiled=True)  28.4 us
    all_to_all x1, blocking collectives, shards(): returned = lax.all_to_all(grads, 'region', 0, 0, tiled=True)  23.4 us
    ppermute x2, starting transfers between devices, passed_along(): return lax.ppermute(block, axis, route)  8.82 us
    pallas_call x1, Pallas kernels, attend_call(): pl.pallas_call(attend_kernel, name='attend', out_shape=jax.ShapeDtypeStru...  7.86 us
    ppermute x2, waiting for transfers between devices, passed_along(): return lax.ppermute(block, axis, route)  5.39 us
    pallas_call x1, Pallas kernels, shards(): pl.pallas_call(project_kernel, name='project', out_shape=jax.ShapeDtypeSt...  4.02 us
    pallas_call x1, Pallas kernels, shards(): pl.pallas_call(return_kernel, name='project_back', out_shape=(jax.ShapeDt...  2.1 us
    pallas_call x1, Pallas kernels, shards(): pl.pallas_call(grad_kernel, name='project_grad', out_shape=jax.ShapeDtype...  2.05 us
  transfers between devices with their start and end apart: 2, of which 1 were waited for; matrix products, arithmetic and copies ran while one was open for 0% of the time, Pallas kernels for 2%

profile of v2, /device:TPU:65, one launch (start us, length us, event | category | flops | bytes accessed | tf_op | source)
XLA Modules:
  0.0 85.2 jit_solution(2954454077375681644)
XLA Ops:
  0.0 0.0 copy-start.3
  0.0 0.8 slice.3
  0.8 6.7 %collective-permute-start = (bf16[1,3,768]{2,1,0:T(4,128)(2,1)S(1)}, bf16[1,3,768]{2,1,0:T(4,128)(2,1)S(1)}, u32[]{:S(2)}, u32[]{:S(2)}) collective-permute-start(bf16[1,3,768]{2,1,0:T(4,128)(2,1)S(1)} %slice.3), channel_id=1, source_target_pairs={{0,1},{1,2},{2,3},{3,4},{4,5},{5,6},{6,7},{8,9},{9,10},{10,11},{11... | collective-permute-start | bytes 13832 | tf_op jit(solution)/shard_map/ppermute | solution.py:27
  8.1 0.0 copy-start.4
  8.1 0.9 %copy-done.4 = bf16[1,128,768]{2,1,0:T(8,128)(2,1)S(1)} copy-done((bf16[1,128,768]{2,1,0:T(8,128)(2,1)S(1)}, bf16[1,128,768]{2,1,0:T(8,128)(2,1)}, u32[]{:S(2)}) %copy-start.4) | copy-done | bytes 196632
  9.0 0.0 copy-start.5
  9.0 2.1 %project_grad.1.grads_hbm = bf16[128,768]{1,0:T(8,128)(2,1)S(1)} custom-call(s32[1,1]{1,0:T(1,128)S(6)} %copy.11.live_ref, bf16[128,768]{1,0:T(8,128)(2,1)S(1)} %bitcast.6, bf16[768,768]{1,0:T(8,128)(2,1)} %wo_hbm.1), custom_call_target="tpu_custom_call" | custom-call | flops 150994944 | bytes 1572864 | tf_op jit(solution)/shard_map/project_grad/pallas_call | solution.py:367
  11.1 0.0 collective-permute-done
  11.1 0.0 copy-done.3
  11.1 0.0 copy-done.5
  11.1 4.0 %project.1 = bf16[32,192,128]{2,1,0:T(8,128)(2,1)} custom-call(s32[1]{0:T(128)} %bitcast.region_ref, s32[1,1]{1,0:T(1,128)S(6)} %copy.11.live_ref, bf16[128,768]{1,0:T(8,128)(2,1)S(1)} %bitcast.5, bf16[3,768]{1,0:T(4,128)(2,1)S(1)} %bitcast.7, bf16[128,768]{1,0:T(8,128)(2,1)S(1)} %project_grad.1.grads_hbm, f32[4,768]{1,0:T(4,128)S(1)} %copy-done.5, ...), custom_call_target="tpu_custom_call" | custom-call | tf_op jit(solution)/shard_map/project/pallas_call | solution.py:383
  15.2 28.4 %all_to_all.10.recv_ref = bf16[32,192,128]{2,1,0:T(8,128)(2,1)S(1)} all-to-all(bf16[32,192,128]{2,1,0:T(8,128)(2,1)} %project.1), channel_id=1, replica_groups=mesh['region'=32,'tm'=8] {'region'}, dimensions={0} | all-to-all | bytes 3145728 | tf_op jit(solution)/shard_map/all_to_all | solution.py:403
  43.5 0.0 copy-start.2
  43.5 7.9 %attend.1 = bf16[32,160,128]{2,1,0:T(8,128)(2,1)S(1)} custom-call(s32[1]{0:T(128)} %bitcast.region_ref, bf16[32,192,128]{2,1,0:T(8,128)(2,1)S(1)} %all_to_all.10.recv_ref), custom_call_target="tpu_custom_call" | custom-call | tf_op jit(solution)/shard_map/attend/pallas_call | solution.py:333
  51.4 0.0 copy-start
  51.4 0.0 copy-start.1
  51.4 23.4 %all_to_all.11.recv_ref = bf16[32,160,128]{2,1,0:T(8,128)(2,1)S(1)} all-to-all(bf16[32,160,128]{2,1,0:T(8,128)(2,1)S(1)} %attend.1), channel_id=1, replica_groups=mesh['region'=32,'tm'=8] {'region'}, dimensions={0} | all-to-all | bytes 2621440 | tf_op jit(solution)/shard_map/all_to_all | solution.py:405
  74.9 0.0 copy-done.2
  74.9 0.0 copy-done
  74.9 0.0 copy-done.1
  74.9 2.1 %project_back.1 = (bf16[128,768]{1,0:T(8,128)(2,1)}, f32[8,768]{1,0:T(8,128)S(1)}, f32[16,768]{1,0:T(8,128)S(1)}) custom-call(s32[1]{0:T(128)} %bitcast.region_ref, s32[1,1]{1,0:T(1,128)S(6)} %copy.11.live_ref, bf16[32,160,128]{2,1,0:T(8,128)(2,1)S(1)} %all_to_all.11.recv_ref, f32[4,768]{1,0:T(4,128)S(1)} %copy-done.5, bf16[768,768]{1,0:T(8,128)(2,1)S(1)} %copy-done, ...), custom_call_target="tpu_custom_call" | custom-call | tf_op jit(solution)/shard_map/project_back/pallas_call | solution.py:406
  77.0 2.2 %collective-permute-start.1 = (f32[8,768]{1,0:T(8,128)S(1)}, f32[8,768]{1,0:T(8,128)S(1)}, u32[]{:S(2)}, u32[]{:S(2)}) collective-permute-start(f32[8,768]{1,0:T(8,128)S(1)} %get-tuple-element.9), channel_id=1, source_target_pairs={{1,0},{2,1},{3,2},{4,3},{5,4},{6,5},{7,6},{9,8},{10,9},{11,10},{12... | collective-permute-start | bytes 73736 | tf_op jit(solution)/shard_map/ppermute | solution.py:27
  79.1 5.4 %collective-permute-done.1.later_ref = f32[8,768]{1,0:T(8,128)S(1)} collective-permute-done((f32[8,768]{1,0:T(8,128)S(1)}, f32[8,768]{1,0:T(8,128)S(1)}, u32[]{:S(2)}, u32[]{:S(2)}) %collective-permute-start.1) | collective-permute-done | bytes 24608 | tf_op jit(solution)/shard_map/ppermute | solution.py:27
  84.5 0.6 finish.1
Async XLA Ops:
  0.0 11.1 %copy-start.3 = (bf16[1,128,768]{2,1,0:T(8,128)(2,1)S(1)}, bf16[1,128,768]{2,1,0:T(8,128)(2,1)}, u32[]{:S(2)}) copy-start(bf16[1,128,768]{2,1,0:T(8,128)(2,1)} %param.8) | copy-start | bytes 589828
  0.8 10.3 %collective-permute-start = (bf16[1,3,768]{2,1,0:T(4,128)(2,1)S(1)}, bf16[1,3,768]{2,1,0:T(4,128)(2,1)S(1)}, u32[]{:S(2)}, u32[]{:S(2)}) collective-permute-start(bf16[1,3,768]{2,1,0:T(4,128)(2,1)S(1)} %slice.3), channel_id=1, source_target_pairs={{0,1},{1,2},{2,3},{3,4},{4,5},{5,6},{6,7},{8,9},{9,10},{10,11},{11... | collective-permute-start | bytes 13832 | tf_op jit(solution)/shard_map/ppermute | solution.py:27
  8.1 0.9 %copy-start.4 = (bf16[1,128,768]{2,1,0:T(8,128)(2,1)S(1)}, bf16[1,128,768]{2,1,0:T(8,128)(2,1)}, u32[]{:S(2)}) copy-start(bf16[1,128,768]{2,1,0:T(8,128)(2,1)} %param.9) | copy-start | bytes 589828
  9.0 2.1 %copy-start.5 = (f32[4,768]{1,0:T(4,128)S(1)}, f32[4,768]{1,0:T(4,128)}, u32[]{:S(2)}) copy-start(f32[4,768]{1,0:T(4,128)} %taps_ref.3) | copy-start | bytes 36868
  43.5 31.3 %copy-start.2 = (bf16[768,768]{1,0:T(8,128)(2,1)S(1)}, bf16[768,768]{1,0:T(8,128)(2,1)}, u32[]{:S(2)}) copy-start(bf16[768,768]{1,0:T(8,128)(2,1)} %wv_ref.1) | copy-start | bytes 3538948
  51.4 23.5 %copy-start = (bf16[768,768]{1,0:T(8,128)(2,1)S(1)}, bf16[768,768]{1,0:T(8,128)(2,1)}, u32[]{:S(2)}) copy-start(bf16[768,768]{1,0:T(8,128)(2,1)} %wq_ref.1) | copy-start | bytes 3538948
  51.4 23.5 %copy-start.1 = (bf16[768,768]{1,0:T(8,128)(2,1)S(1)}, bf16[768,768]{1,0:T(8,128)(2,1)}, u32[]{:S(2)}) copy-start(bf16[768,768]{1,0:T(8,128)(2,1)} %wk_ref.1) | copy-start | bytes 3538948
  77.0 7.6 %collective-permute-start.1 = (f32[8,768]{1,0:T(8,128)S(1)}, f32[8,768]{1,0:T(8,128)S(1)}, u32[]{:S(2)}, u32[]{:S(2)}) collective-permute-start(f32[8,768]{1,0:T(8,128)S(1)} %get-tuple-element.9), channel_id=1, source_target_pairs={{1,0},{2,1},{3,2},{4,3},{5,4},{6,5},{7,6},{9,8},{10,9},{11,10},{12... | collective-permute-start | bytes 73736 | tf_op jit(solution)/shard_map/ppermute | solution.py:27

commit v3 on v2

--- a/solution.py
+++ b/solution.py
@@ -16,7 +16,7 @@
 QUERY_STEP = 1024
 QUERY_WIDTHS = (512, 640, 768, 896, 1024)
 MASKED = -1e30
-HEADS_STEP = 4
+HEADS_STEP = 6
 BF16 = jnp.bfloat16
 F32 = jnp.float32
 

time: 85.4 us -> 85.5 us (level)
  Pallas kernels: 16.7 us -> 14.6 us
  waiting for transfers between devices: 5.39 us -> 6.93 us
    pallas_call x1, Pallas kernels: 7.86 us -> 5.81 us  [attend_call(): pl.pallas_call(attend_kernel, name='attend', out_shape=jax.ShapeDtypeStru...]
    ppermute x2, waiting for transfers between devices: 5.39 us -> 6.93 us  [passed_along(): return lax.ppermute(block, axis, route)]
where the time goes in v3:
time: 85.5 us; the launch traced here: 84.6 us
  blocking collectives  52.1 us (61%)
  Pallas kernels  14.6 us (17%)
  starting transfers between devices  8.57 us (10%)
  waiting for transfers between devices  6.93 us (8%)
  local copies, waits for them, and re-layouts  1.73 us (2%)
    all_to_all x1, blocking collectives, shards(): gathered = lax.all_to_all(sent, 'region', 0, 0, tiled=True)  28.4 us
    all_to_all x1, blocking collectives, shards(): returned = lax.all_to_all(grads, 'region', 0, 0, tiled=True)  23.7 us
    ppermute x2, starting transfers between devices, passed_along(): return lax.ppermute(block, axis, route)  8.57 us
    ppermute x2, waiting for transfers between devices, passed_along(): return lax.ppermute(block, axis, route)  6.93 us
    pallas_call x1, Pallas kernels, attend_call(): pl.pallas_call(attend_kernel, name='attend', out_shape=jax.ShapeDtypeStru...  5.81 us
    pallas_call x1, Pallas kernels, shards(): pl.pallas_call(project_kernel, name='project', out_shape=jax.ShapeDtypeSt...  4.01 us
    pallas_call x1, Pallas kernels, shards(): pl.pallas_call(return_kernel, name='project_back', out_shape=(jax.ShapeDt...  2.1 us
    pallas_call x1, Pallas kernels, shards(): pl.pallas_call(grad_kernel, name='project_grad', out_shape=jax.ShapeDtype...  2.05 us
  transfers between devices with their start and end apart: 2, of which 1 were waited for; matrix products, arithmetic and copies ran while one was open for 0% of the time, Pallas kernels for 2%

profile of v3, /device:TPU:65, one launch (start us, length us, event | category | flops | bytes accessed | tf_op | source)
XLA Modules:
  0.0 84.6 jit_solution(4161522754272689985)
XLA Ops:
  0.0 0.0 copy-start.3
  0.0 0.8 slice.3
  0.8 6.7 %collective-permute-start = (bf16[1,3,768]{2,1,0:T(4,128)(2,1)S(1)}, bf16[1,3,768]{2,1,0:T(4,128)(2,1)S(1)}, u32[]{:S(2)}, u32[]{:S(2)}) collective-permute-start(bf16[1,3,768]{2,1,0:T(4,128)(2,1)S(1)} %slice.3), channel_id=1, source_target_pairs={{0,1},{1,2},{2,3},{3,4},{4,5},{5,6},{6,7},{8,9},{9,10},{10,11},{11... | collective-permute-start | bytes 13832 | tf_op jit(solution)/shard_map/ppermute | solution.py:27
  8.1 0.0 copy-start.4
  8.1 0.9 %copy-done.4 = bf16[1,128,768]{2,1,0:T(8,128)(2,1)S(1)} copy-done((bf16[1,128,768]{2,1,0:T(8,128)(2,1)S(1)}, bf16[1,128,768]{2,1,0:T(8,128)(2,1)}, u32[]{:S(2)}) %copy-start.4) | copy-done | bytes 196632
  9.0 0.0 copy-start.5
  9.0 2.1 %project_grad.1.grads_hbm = bf16[128,768]{1,0:T(8,128)(2,1)S(1)} custom-call(s32[1,1]{1,0:T(1,128)S(6)} %copy.11.live_ref, bf16[128,768]{1,0:T(8,128)(2,1)S(1)} %bitcast.6, bf16[768,768]{1,0:T(8,128)(2,1)} %wo_hbm.1), custom_call_target="tpu_custom_call" | custom-call | flops 150994944 | bytes 1572864 | tf_op jit(solution)/shard_map/project_grad/pallas_call | solution.py:367
  11.1 0.0 collective-permute-done
  11.1 0.0 copy-done.3
  11.1 0.0 copy-done.5
  11.1 4.0 %project.1 = bf16[32,192,128]{2,1,0:T(8,128)(2,1)} custom-call(s32[1]{0:T(128)} %bitcast.region_ref, s32[1,1]{1,0:T(1,128)S(6)} %copy.11.live_ref, bf16[128,768]{1,0:T(8,128)(2,1)S(1)} %bitcast.5, bf16[3,768]{1,0:T(4,128)(2,1)S(1)} %bitcast.7, bf16[128,768]{1,0:T(8,128)(2,1)S(1)} %project_grad.1.grads_hbm, f32[4,768]{1,0:T(4,128)S(1)} %copy-done.5, ...), custom_call_target="tpu_custom_call" | custom-call | tf_op jit(solution)/shard_map/project/pallas_call | solution.py:383
  15.2 28.4 %all_to_all.10.recv_ref = bf16[32,192,128]{2,1,0:T(8,128)(2,1)S(1)} all-to-all(bf16[32,192,128]{2,1,0:T(8,128)(2,1)} %project.1), channel_id=1, replica_groups=mesh['region'=32,'tm'=8] {'region'}, dimensions={0} | all-to-all | bytes 3145728 | tf_op jit(solution)/shard_map/all_to_all | solution.py:403
  43.5 0.0 copy-start.2
  43.5 5.8 %attend.1 = bf16[32,160,128]{2,1,0:T(8,128)(2,1)S(1)} custom-call(s32[1]{0:T(128)} %bitcast.region_ref, bf16[32,192,128]{2,1,0:T(8,128)(2,1)S(1)} %all_to_all.10.recv_ref), custom_call_target="tpu_custom_call" | custom-call | tf_op jit(solution)/shard_map/attend/pallas_call | solution.py:333
  49.3 0.0 copy-start
  49.4 0.0 copy-start.1
  49.4 23.7 %all_to_all.11.recv_ref = bf16[32,160,128]{2,1,0:T(8,128)(2,1)S(1)} all-to-all(bf16[32,160,128]{2,1,0:T(8,128)(2,1)S(1)} %attend.1), channel_id=1, replica_groups=mesh['region'=32,'tm'=8] {'region'}, dimensions={0} | all-to-all | bytes 2621440 | tf_op jit(solution)/shard_map/all_to_all | solution.py:405
  73.1 0.0 copy-done.2
  73.1 0.0 copy-done
  73.1 0.0 copy-done.1
  73.1 2.1 %project_back.1 = (bf16[128,768]{1,0:T(8,128)(2,1)}, f32[8,768]{1,0:T(8,128)S(1)}, f32[16,768]{1,0:T(8,128)S(1)}) custom-call(s32[1]{0:T(128)} %bitcast.region_ref, s32[1,1]{1,0:T(1,128)S(6)} %copy.11.live_ref, bf16[32,160,128]{2,1,0:T(8,128)(2,1)S(1)} %all_to_all.11.recv_ref, f32[4,768]{1,0:T(4,128)S(1)} %copy-done.5, bf16[768,768]{1,0:T(8,128)(2,1)S(1)} %copy-done, ...), custom_call_target="tpu_custom_call" | custom-call | tf_op jit(solution)/shard_map/project_back/pallas_call | solution.py:406
  75.2 1.9 %collective-permute-start.1 = (f32[8,768]{1,0:T(8,128)S(1)}, f32[8,768]{1,0:T(8,128)S(1)}, u32[]{:S(2)}, u32[]{:S(2)}) collective-permute-start(f32[8,768]{1,0:T(8,128)S(1)} %get-tuple-element.9), channel_id=1, source_target_pairs={{1,0},{2,1},{3,2},{4,3},{5,4},{6,5},{7,6},{9,8},{10,9},{11,10},{12... | collective-permute-start | bytes 73736 | tf_op jit(solution)/shard_map/ppermute | solution.py:27
  77.1 6.9 %collective-permute-done.1.later_ref = f32[8,768]{1,0:T(8,128)S(1)} collective-permute-done((f32[8,768]{1,0:T(8,128)S(1)}, f32[8,768]{1,0:T(8,128)S(1)}, u32[]{:S(2)}, u32[]{:S(2)}) %collective-permute-start.1) | collective-permute-done | bytes 24608 | tf_op jit(solution)/shard_map/ppermute | solution.py:27
  84.0 0.6 finish.1
Async XLA Ops:
  0.0 11.1 %copy-start.3 = (bf16[1,128,768]{2,1,0:T(8,128)(2,1)S(1)}, bf16[1,128,768]{2,1,0:T(8,128)(2,1)}, u32[]{:S(2)}) copy-start(bf16[1,128,768]{2,1,0:T(8,128)(2,1)} %param.8) | copy-start | bytes 589828
  0.8 10.3 %collective-permute-start = (bf16[1,3,768]{2,1,0:T(4,128)(2,1)S(1)}, bf16[1,3,768]{2,1,0:T(4,128)(2,1)S(1)}, u32[]{:S(2)}, u32[]{:S(2)}) collective-permute-start(bf16[1,3,768]{2,1,0:T(4,128)(2,1)S(1)} %slice.3), channel_id=1, source_target_pairs={{0,1},{1,2},{2,3},{3,4},{4,5},{5,6},{6,7},{8,9},{9,10},{10,11},{11... | collective-permute-start | bytes 13832 | tf_op jit(solution)/shard_map/ppermute | solution.py:27
  8.1 0.9 %copy-start.4 = (bf16[1,128,768]{2,1,0:T(8,128)(2,1)S(1)}, bf16[1,128,768]{2,1,0:T(8,128)(2,1)}, u32[]{:S(2)}) copy-start(bf16[1,128,768]{2,1,0:T(8,128)(2,1)} %param.9) | copy-start | bytes 589828
  9.0 2.1 %copy-start.5 = (f32[4,768]{1,0:T(4,128)S(1)}, f32[4,768]{1,0:T(4,128)}, u32[]{:S(2)}) copy-start(f32[4,768]{1,0:T(4,128)} %taps_ref.3) | copy-start | bytes 36868
  43.5 29.5 %copy-start.2 = (bf16[768,768]{1,0:T(8,128)(2,1)S(1)}, bf16[768,768]{1,0:T(8,128)(2,1)}, u32[]{:S(2)}) copy-start(bf16[768,768]{1,0:T(8,128)(2,1)} %wv_ref.1) | copy-start | bytes 3538948
  49.3 23.7 %copy-start = (bf16[768,768]{1,0:T(8,128)(2,1)S(1)}, bf16[768,768]{1,0:T(8,128)(2,1)}, u32[]{:S(2)}) copy-start(bf16[768,768]{1,0:T(8,128)(2,1)} %wq_ref.1) | copy-start | bytes 3538948
  49.4 23.7 %copy-start.1 = (bf16[768,768]{1,0:T(8,128)(2,1)S(1)}, bf16[768,768]{1,0:T(8,128)(2,1)}, u32[]{:S(2)}) copy-start(bf16[768,768]{1,0:T(8,128)(2,1)} %wk_ref.1) | copy-start | bytes 3538948
  75.2 8.8 %collective-permute-start.1 = (f32[8,768]{1,0:T(8,128)S(1)}, f32[8,768]{1,0:T(8,128)S(1)}, u32[]{:S(2)}, u32[]{:S(2)}) collective-permute-start(f32[8,768]{1,0:T(8,128)S(1)} %get-tuple-element.9), channel_id=1, source_target_pairs={{1,0},{2,1},{3,2},{4,3},{5,4},{6,5},{7,6},{9,8},{10,9},{11,10},{12... | collective-permute-start | bytes 73736 | tf_op jit(solution)/shard_map/ppermute | solution.py:27

commit v4 on v3

--- a/solution.py
+++ b/solution.py
@@ -104,10 +104,11 @@
     given = grads_ref[...]
     leaving = []
     for step in range(steps):
-        for move in weights[step]:
-            move.wait()
+        weights[step][0].wait()
         queries = (times(hidden, wq_ref[step]).astype(BF16).astype(F32) * (1.0 / math.sqrt(HD))).astype(BF16)
+        weights[step][1].wait()
         keys = jnp.where(alive, times(hidden, wk_ref[step]), jnp.nan).astype(BF16)
+        weights[step][2].wait()
         values = jnp.where(alive, times(hidden, wv_ref[step]), jnp.nan).astype(BF16)
         grads = given[:, step * columns : (step + 1) * columns]
         for head in range(HEADS_STEP):

time: 85.5 us -> 86.2 us (level)
  no operation moved by 1% of the time
where the time goes in v4:
time: 86.2 us; the launch traced here: 85.4 us
  blocking collectives  52.1 us (60%)
  Pallas kernels  15.1 us (18%)
  starting transfers between devices  8.57 us (10%)
  waiting for transfers between devices  7.19 us (8%)
  local copies, waits for them, and re-layouts  1.73 us (2%)
    all_to_all x1, blocking collectives, shards(): gathered = lax.all_to_all(sent, 'region', 0, 0, tiled=True)  28.4 us
    all_to_all x1, blocking collectives, shards(): returned = lax.all_to_all(grads, 'region', 0, 0, tiled=True)  23.7 us
    ppermute x2, starting transfers between devices, passed_along(): return lax.ppermute(block, axis, route)  8.57 us
    ppermute x2, waiting for transfers between devices, passed_along(): return lax.ppermute(block, axis, route)  7.19 us
    pallas_call x1, Pallas kernels, attend_call(): pl.pallas_call(attend_kernel, name='attend', out_shape=jax.ShapeDtypeStru...  5.99 us
    pallas_call x1, Pallas kernels, shards(): pl.pallas_call(project_kernel, name='project', out_shape=jax.ShapeDtypeSt...  4.32 us
    pallas_call x1, Pallas kernels, shards(): pl.pallas_call(return_kernel, name='project_back', out_shape=(jax.ShapeDt...  2.11 us
    pallas_call x1, Pallas kernels, shards(): pl.pallas_call(grad_kernel, name='project_grad', out_shape=jax.ShapeDtype...  2.06 us
  transfers between devices with their start and end apart: 2, of which 1 were waited for; matrix products, arithmetic and copies ran while one was open for 0% of the time, Pallas kernels for 2%

profile of v4, /device:TPU:65, one launch (start us, length us, event | category | flops | bytes accessed | tf_op | source)
XLA Modules:
  0.0 85.4 jit_solution(14792538467209948320)
XLA Ops:
  0.0 0.0 copy-start.3
  0.0 0.8 slice.3
  0.8 6.7 %collective-permute-start = (bf16[1,3,768]{2,1,0:T(4,128)(2,1)S(1)}, bf16[1,3,768]{2,1,0:T(4,128)(2,1)S(1)}, u32[]{:S(2)}, u32[]{:S(2)}) collective-permute-start(bf16[1,3,768]{2,1,0:T(4,128)(2,1)S(1)} %slice.3), channel_id=1, source_target_pairs={{0,1},{1,2},{2,3},{3,4},{4,5},{5,6},{6,7},{8,9},{9,10},{10,11},{11... | collective-permute-start | bytes 13832 | tf_op jit(solution)/shard_map/ppermute | solution.py:27
  8.1 0.0 copy-start.4
  8.1 0.9 %copy-done.4 = bf16[1,128,768]{2,1,0:T(8,128)(2,1)S(1)} copy-done((bf16[1,128,768]{2,1,0:T(8,128)(2,1)S(1)}, bf16[1,128,768]{2,1,0:T(8,128)(2,1)}, u32[]{:S(2)}) %copy-start.4) | copy-done | bytes 196632
  9.0 0.0 copy-start.5
  9.0 2.1 %project_grad.1.grads_hbm = bf16[128,768]{1,0:T(8,128)(2,1)S(1)} custom-call(s32[1,1]{1,0:T(1,128)S(6)} %copy.11.live_ref, bf16[128,768]{1,0:T(8,128)(2,1)S(1)} %bitcast.6, bf16[768,768]{1,0:T(8,128)(2,1)} %wo_hbm.1), custom_call_target="tpu_custom_call" | custom-call | flops 150994944 | bytes 1572864 | tf_op jit(solution)/shard_map/project_grad/pallas_call | solution.py:368
  11.1 0.0 collective-permute-done
  11.1 0.0 copy-done.3
  11.1 0.0 copy-done.5
  11.1 4.3 %project.1 = bf16[32,192,128]{2,1,0:T(8,128)(2,1)} custom-call(s32[1]{0:T(128)} %bitcast.region_ref, s32[1,1]{1,0:T(1,128)S(6)} %copy.11.live_ref, bf16[128,768]{1,0:T(8,128)(2,1)S(1)} %bitcast.5, bf16[3,768]{1,0:T(4,128)(2,1)S(1)} %bitcast.7, bf16[128,768]{1,0:T(8,128)(2,1)S(1)} %project_grad.1.grads_hbm, f32[4,768]{1,0:T(4,128)S(1)} %copy-done.5, ...), custom_call_target="tpu_custom_call" | custom-call | tf_op jit(solution)/shard_map/project/pallas_call | solution.py:384
  15.5 28.4 %all_to_all.10.recv_ref = bf16[32,192,128]{2,1,0:T(8,128)(2,1)S(1)} all-to-all(bf16[32,192,128]{2,1,0:T(8,128)(2,1)} %project.1), channel_id=1, replica_groups=mesh['region'=32,'tm'=8] {'region'}, dimensions={0} | all-to-all | bytes 3145728 | tf_op jit(solution)/shard_map/all_to_all | solution.py:404
  43.8 0.0 copy-start.2
  43.8 6.0 %attend.1 = bf16[32,160,128]{2,1,0:T(8,128)(2,1)S(1)} custom-call(s32[1]{0:T(128)} %bitcast.region_ref, bf16[32,192,128]{2,1,0:T(8,128)(2,1)S(1)} %all_to_all.10.recv_ref), custom_call_target="tpu_custom_call" | custom-call | tf_op jit(solution)/shard_map/attend/pallas_call | solution.py:334
  49.8 0.0 copy-start
  49.8 0.0 copy-start.1
  49.9 23.7 %all_to_all.11.recv_ref = bf16[32,160,128]{2,1,0:T(8,128)(2,1)S(1)} all-to-all(bf16[32,160,128]{2,1,0:T(8,128)(2,1)S(1)} %attend.1), channel_id=1, replica_groups=mesh['region'=32,'tm'=8] {'region'}, dimensions={0} | all-to-all | bytes 2621440 | tf_op jit(solution)/shard_map/all_to_all | solution.py:406
  73.6 0.0 copy-done.2
  73.6 0.0 copy-done
  73.6 0.0 copy-done.1
  73.6 2.1 %project_back.1 = (bf16[128,768]{1,0:T(8,128)(2,1)}, f32[8,768]{1,0:T(8,128)S(1)}, f32[16,768]{1,0:T(8,128)S(1)}) custom-call(s32[1]{0:T(128)} %bitcast.region_ref, s32[1,1]{1,0:T(1,128)S(6)} %copy.11.live_ref, bf16[32,160,128]{2,1,0:T(8,128)(2,1)S(1)} %all_to_all.11.recv_ref, f32[4,768]{1,0:T(4,128)S(1)} %copy-done.5, bf16[768,768]{1,0:T(8,128)(2,1)S(1)} %copy-done, ...), custom_call_target="tpu_custom_call" | custom-call | tf_op jit(solution)/shard_map/project_back/pallas_call | solution.py:407
  75.7 1.9 %collective-permute-start.1 = (f32[8,768]{1,0:T(8,128)S(1)}, f32[8,768]{1,0:T(8,128)S(1)}, u32[]{:S(2)}, u32[]{:S(2)}) collective-permute-start(f32[8,768]{1,0:T(8,128)S(1)} %get-tuple-element.9), channel_id=1, source_target_pairs={{1,0},{2,1},{3,2},{4,3},{5,4},{6,5},{7,6},{9,8},{10,9},{11,10},{12... | collective-permute-start | bytes 73736 | tf_op jit(solution)/shard_map/ppermute | solution.py:27
  77.6 7.2 %collective-permute-done.1.later_ref = f32[8,768]{1,0:T(8,128)S(1)} collective-permute-done((f32[8,768]{1,0:T(8,128)S(1)}, f32[8,768]{1,0:T(8,128)S(1)}, u32[]{:S(2)}, u32[]{:S(2)}) %collective-permute-start.1) | collective-permute-done | bytes 24608 | tf_op jit(solution)/shard_map/ppermute | solution.py:27
  84.8 0.6 finish.1
Async XLA Ops:
  0.0 11.1 %copy-start.3 = (bf16[1,128,768]{2,1,0:T(8,128)(2,1)S(1)}, bf16[1,128,768]{2,1,0:T(8,128)(2,1)}, u32[]{:S(2)}) copy-start(bf16[1,128,768]{2,1,0:T(8,128)(2,1)} %param.8) | copy-start | bytes 589828
  0.8 10.3 %collective-permute-start = (bf16[1,3,768]{2,1,0:T(4,128)(2,1)S(1)}, bf16[1,3,768]{2,1,0:T(4,128)(2,1)S(1)}, u32[]{:S(2)}, u32[]{:S(2)}) collective-permute-start(bf16[1,3,768]{2,1,0:T(4,128)(2,1)S(1)} %slice.3), channel_id=1, source_target_pairs={{0,1},{1,2},{2,3},{3,4},{4,5},{5,6},{6,7},{8,9},{9,10},{10,11},{11... | collective-permute-start | bytes 13832 | tf_op jit(solution)/shard_map/ppermute | solution.py:27
  8.1 0.9 %copy-start.4 = (bf16[1,128,768]{2,1,0:T(8,128)(2,1)S(1)}, bf16[1,128,768]{2,1,0:T(8,128)(2,1)}, u32[]{:S(2)}) copy-start(bf16[1,128,768]{2,1,0:T(8,128)(2,1)} %param.9) | copy-start | bytes 589828
  9.0 2.1 %copy-start.5 = (f32[4,768]{1,0:T(4,128)S(1)}, f32[4,768]{1,0:T(4,128)}, u32[]{:S(2)}) copy-start(f32[4,768]{1,0:T(4,128)} %taps_ref.3) | copy-start | bytes 36868
  43.8 29.7 %copy-start.2 = (bf16[768,768]{1,0:T(8,128)(2,1)S(1)}, bf16[768,768]{1,0:T(8,128)(2,1)}, u32[]{:S(2)}) copy-start(bf16[768,768]{1,0:T(8,128)(2,1)} %wv_ref.1) | copy-start | bytes 3538948
  49.8 23.7 %copy-start = (bf16[768,768]{1,0:T(8,128)(2,1)S(1)}, bf16[768,768]{1,0:T(8,128)(2,1)}, u32[]{:S(2)}) copy-start(bf16[768,768]{1,0:T(8,128)(2,1)} %wq_ref.1) | copy-start | bytes 3538948
  49.8 23.7 %copy-start.1 = (bf16[768,768]{1,0:T(8,128)(2,1)S(1)}, bf16[768,768]{1,0:T(8,128)(2,1)}, u32[]{:S(2)}) copy-start(bf16[768,768]{1,0:T(8,128)(2,1)} %wk_ref.1) | copy-start | bytes 3538948
  75.7 9.1 %collective-permute-start.1 = (f32[8,768]{1,0:T(8,128)S(1)}, f32[8,768]{1,0:T(8,128)S(1)}, u32[]{:S(2)}, u32[]{:S(2)}) collective-permute-start(f32[8,768]{1,0:T(8,128)S(1)} %get-tuple-element.9), channel_id=1, source_target_pairs={{1,0},{2,1},{3,2},{4,3},{5,4},{6,5},{7,6},{9,8},{10,9},{11,10},{12... | collective-permute-start | bytes 73736 | tf_op jit(solution)/shard_map/ppermute | solution.py:27
